TPU v7x, 128 devices: a whole 4x4x4 slice. The times are simulated.
128 devices in a mesh: dp: 4 (over x), tensor: 2 (over core), expert: 16 (over z, y).
Axes of the slice: x: 4, y: 4, z: 4, core: 2. Of those that a mesh axis runs over, the one named last changes fastest.
Arguments:
- tokens: bfloat16 [8192, 2304], P(('dp', 'tensor', 'expert')), may hold values from -6 to 6
- routes: int32 [8192, 2], P(('dp', 'tensor', 'expert')), may hold values from 0 to 7, all different within a row; in each aligned block of 64 rows (0 to 63, 64 to 127, ...) at most 24 rows name the same one
- gates: float32 [8192, 2], P(('dp', 'tensor', 'expert')), may hold values from 0.2 to 1
- segments: int32 [8192], P(('dp', 'tensor', 'expert')), may hold values from 0 to 31, never falling along the last dimension, each value on 1 to 512 neighbouring positions
- w_gate: bfloat16 [16, 2304, 3840], P('expert', None, ('dp', 'tensor')), may hold values from -0.125 to 0.125
- w_up: bfloat16 [16, 2304, 3840], P('expert', None, ('dp', 'tensor')), may hold values from -0.125 to 0.125
- w_down: bfloat16 [16, 3840, 2304], P('expert', ('dp', 'tensor')), may hold values from -0.0625 to 0.0625
Outputs:
- embedded: bfloat16 [8192, 2304], P(('dp', 'tensor', 'expert'))
- pooled: float32 [32, 2304], replicated
Inputs may be any that keep to these rules, and one draw needn't show every extreme that they name: `routes`: each residue names two different experts. Within the rows of one device no expert is named more than 24 times, and in every draw some expert is named exactly 24 times by the rows of some device. `segments`: sequence numbers never fall along the residues; each sequence has 1 to 512 residues and one has exactly 512.
All inputs are finite; a program needn't handle non-finite values.
Results may differ from a plain program's by a relative error of at most 0.0085.
Values may be sent and summed in bfloat16 or wider, within the bound.
A program may use at most 64 MiB of HBM per device.

v0:
```python
import jax
import jax.numpy as jnp
from jax import lax
from jax.sharding import PartitionSpec as P

EXPERTS = 8
TOP = 2
CAP = 24


epsilon = 1e-06


def norm_tokens(tokens):
    values = tokens.astype(jnp.float32)
    scale = lax.rsqrt(jnp.mean(values * values, axis=1, keepdims=True) + epsilon)
    return (values, (values * scale).astype(jnp.bfloat16))


def slot_numbers(routes):
    flat_routes = routes.reshape(-1)
    onehot = (flat_routes[:, None] == jnp.arange(EXPERTS, dtype=jnp.int32)[None, :]).astype(
        jnp.int32
    )
    before = jnp.cumsum(onehot, axis=0) - onehot
    slot_rank = jnp.sum(before * onehot, axis=1)
    return flat_routes * CAP + slot_rank


def placement_matrix(slot_index, tok_count):
    hits = (jnp.arange(EXPERTS * CAP, dtype=jnp.int32)[:, None] == slot_index[None, :]).astype(
        jnp.int32
    )
    return jnp.sum(hits.reshape(EXPERTS * CAP, tok_count, TOP), axis=2).astype(jnp.bfloat16)


def fan_out(slot_rows, replicas):
    leading = slot_rows.shape[:-2]
    features = slot_rows.shape[-1]
    shaped = slot_rows.reshape(leading + (EXPERTS, CAP, features))
    shaped = jnp.repeat(shaped, replicas, axis=len(leading))
    return shaped.reshape(leading + (EXPERTS * replicas * CAP, features))


def expert_hidden(row_block, w_gate, w_up):
    gate_proj = jnp.einsum("nacd,adf->nacf", row_block, w_gate, preferred_element_type=jnp.float32)
    up_proj = jnp.einsum("nacd,adf->nacf", row_block, w_up, preferred_element_type=jnp.float32)
    return (jax.nn.silu(gate_proj) * up_proj).astype(jnp.bfloat16)


def shards(tokens, routes, gates, segments, w_gate, w_up, w_down):
    tok_count = tokens.shape[0]
    width = tokens.shape[1]
    experts_axis = lax.axis_size("expert")
    per_device = w_gate.shape[0]
    replicas = max(1, experts_axis // EXPERTS)
    plane = lax.axis_size("dp") * lax.axis_size("tensor")
    values, normed = norm_tokens(tokens)
    slot_index = slot_numbers(routes)
    placing = placement_matrix(slot_index, tok_count)
    slot_rows = jnp.dot(placing, normed, preferred_element_type=jnp.float32).astype(jnp.bfloat16)
    send_rows = fan_out(slot_rows, replicas)
    received = lax.all_to_all(send_rows, "expert", split_axis=0, concat_axis=0, tiled=True)
    local_rows = received.reshape(experts_axis, per_device, CAP, width)
    hidden = expert_hidden(
        lax.all_gather(local_rows, ("dp", "tensor"), axis=0, tiled=True), w_gate, w_up
    )
    summed = lax.psum_scatter(
        jnp.einsum("nacf,afd->nacd", hidden, w_down, preferred_element_type=jnp.float32).astype(
            jnp.bfloat16
        ),
        ("dp", "tensor"),
        scatter_dimension=0,
        tiled=True,
    )
    returned = lax.all_to_all(summed, "expert", split_axis=0, concat_axis=0, tiled=True).astype(
        jnp.float32
    )
    expert_out = jnp.sum(returned.reshape(EXPERTS, replicas, CAP, width), axis=1)
    picked = jnp.take(expert_out.reshape(EXPERTS * CAP, width), slot_index, axis=0).reshape(
        tok_count, TOP, width
    )
    mixed = values + jnp.sum(gates[:, :, None] * picked, axis=1)
    embedded = mixed.astype(jnp.bfloat16)
    devices_all = plane * experts_axis
    seq_total = tok_count * devices_all // 256
    seq_hot = (jnp.arange(seq_total, dtype=jnp.int32)[:, None] == segments[None, :]).astype(
        jnp.bfloat16
    )
    seq_sums = jnp.dot(seq_hot, embedded, preferred_element_type=jnp.float32)
    seq_counts = jnp.sum(seq_hot.astype(jnp.float32), axis=1)
    total_sums, total_counts = lax.psum((seq_sums, seq_counts), ("dp", "tensor", "expert"))
    pooled = total_sums / total_counts[:, None]
    return (embedded, pooled)


def solution(mesh):
    placed = (
        P(("dp", "tensor", "expert"), None),
        P(("dp", "tensor", "expert"), None),
        P(("dp", "tensor", "expert"), None),
        P(("dp", "tensor", "expert")),
        P("expert", None, ("dp", "tensor")),
        P("expert", None, ("dp", "tensor")),
        P("expert", ("dp", "tensor"), None),
    )
    return jax.shard_map(
        shards,
        mesh=mesh,
        in_specs=placed,
        out_specs=(P(("dp", "tensor", "expert"), None), P()),
        check_vma=False,
    )
```

profile of v0, /device:TPU:1, one launch (start us, length us, event | category | flops | bytes accessed | tf_op | source)
XLA Modules:
  0.0 430.2 jit_solution(17965702247409334811)
XLA Ops:
  7.2 0.9 copy.33
  8.1 0.1 reshape.117
  8.4 0.2 reduce_window_sum.11
  8.5 0.2 select_reduce_fusion
  8.7 0.1 reduce_sum.59
  8.9 0.7 compare_and_fusion
  9.7 1.1 fusion.9
  10.9 1.4 convolution_convert_fusion
  12.3 0.1 broadcast_in_dim.13
  12.4 32.4 %all_to_all.14 = bf16[16,24,2304]{2,1,0:T(8,128)(2,1)S(1)} all-to-all(bf16[16,24,2304]{2,1,0:T(8,128)(2,1)S(1)} %bitcast.63), channel_id=1, replica_groups=mesh['dp'=4,'tensor'=2,'expert'=16] {'expert'}, dimensions={0} | all-to-all | bytes 3538944 | tf_op jit(solution)/shard_map/all_to_all | solution.py:63
  44.8 1.5 copy.36
  46.4 73.1 %all-gather.3.cloned.1.call-done = bf16[128,24,2304]{2,0,1:T(8,128)(2,1)} async-done(((bf16[16,24,2304]{2,0,1:T(8,128)(2,1)}), bf16[128,24,2304]{2,0,1:T(8,128)(2,1)}) %all-gather.3.cloned.1.call-update) | async-done | bytes 14155792 | tf_op jit(solution)/shard_map/all_gather | solution.py:66
  119.5 11.4 %fusion.6 = f32[128,24,480]{0,2,1:T(8,128)S(1)} fusion(bf16[128,24,2304]{2,0,1:T(8,128)(2,1)} %all-gather.3.cloned.1.call-done, bf16[1,2304,480]{1,2,0:T(8,128)(2,1)} %param.12), kind=kOutput, calls=%fused_computation.13 | convolution fusion | flops 6794772480 | bytes 22265856 | tf_op jit(solution)/shard_map/nacd,adf->nacf/dot_general | solution.py:47
  130.9 8.1 %fusion = bf16[128,1,24,480]{0,3,2,1:T(8,128)(2,1)S(1)} fusion(f32[128,24,480]{0,2,1:T(8,128)S(1)} %fusion.6, bf16[128,24,2304]{2,0,1:T(8,128)(2,1)S(1)} %copy-done.5, bf16[1,2304,480]{1,2,0:T(8,128)(2,1)S(1)} %copy-done.6), kind=kOutput, calls=%fused_computation.3 | convolution fusion | flops 6803619840 | bytes 25214976 | tf_op jit(solution)/shard_map/nacd,adf->nacf/dot_general | solution.py:46
  139.0 10.3 %convert_bitcast_fusion = bf16[128,1,24,2304]{3,0,2,1:T(8,128)(2,1)} fusion(bf16[128,1,24,480]{0,3,2,1:T(8,128)(2,1)S(1)} %fusion, bf16[1,480,2304]{2,1,0:T(8,128)(2,1)S(1)} %copy-done), kind=kOutput, calls=%fused_computation.1 | convolution fusion | flops 6801850368 | bytes 19316736 | tf_op jit(solution)/shard_map/nacf,afd->nacd/dot_general | solution.py:69
  149.3 79.5 %reduce-scatter.2.cloned.1.call-done = bf16[16,1,24,2304]{3,0,2,1:T(8,128)(2,1)} async-done(((bf16[128,1,24,2304]{3,0,2,1:T(8,128)(2,1)}), bf16[16,1,24,2304]{3,0,2,1:T(8,128)(2,1)}) %reduce-scatter.2.cloned.1.call-update) | async-done | bytes 1769488 | tf_op jit(solution)/shard_map/reduce_scatter | solution.py:68
  228.8 3.2 copy.37
  232.0 6.9 %all-to-all-start.1 = ((bf16[16,1,24,2304]{3,2,1,0:T(8,128)(2,1)}), bf16[16,1,24,2304]{3,2,1,0:T(8,128)(2,1)}, u32[]{:S(2)}, u32[]{:S(2)}) async-start(bf16[16,1,24,2304]{3,2,1,0:T(8,128)(2,1)} %copy.37), calls=%async_computation.2 | async-start | bytes 3538944 | tf_op jit(solution)/shard_map/all_to_all | solution.py:76
  238.9 0.2 all-reduce.2.cloned.1.call-start
  239.2 0.1 mul.61
  239.3 0.1 copy.35
  239.6 23.3 %all-to-all-done.1 = bf16[16,1,24,2304]{3,2,1,0:T(8,128)(2,1)} async-done(((bf16[16,1,24,2304]{3,2,1,0:T(8,128)(2,1)}), bf16[16,1,24,2304]{3,2,1,0:T(8,128)(2,1)}, u32[]{:S(2)}, u32[]{:S(2)}) %all-to-all-start.1) | async-done | bytes 1769504 | tf_op jit(solution)/shard_map/all_to_all | solution.py:76
  262.9 3.2 convert_reduce_fusion
  266.0 4.0 gather_fusion
  270.0 2.0 gather.7
  272.0 3.2 multiply_reduce_fusion
  275.3 1.0 fusion.11
  276.3 0.9 fusion.17
  277.2 0.1 convert_reduce_fusion.2
  277.4 68.6 %psum.15 = f32[32]{0:T(128)S(1)} all-reduce(f32[32]{0:T(128)S(1)} %convert_reduce_fusion.2), channel_id=1, replica_groups=mesh['dp'=4,'tensor'=2,'expert'=16] {'dp','tensor','expert'}, use_global_device_ids=true, to_apply=%region_9.10 | all-reduce | flops 32 | bytes 256 | tf_op jit(solution)/shard_map/psum | solution.py:92
  346.0 75.9 %all-reduce.2.cloned.1.call-done = f32[32,2304]{1,0:T(8,128)} async-done(((f32[32,2304]{1,0:T(8,128)}), f32[32,2304]{1,0:T(8,128)}) %all-reduce.2.cloned.1.call-update) | async-done | bytes 294928 | tf_op jit(solution)/shard_map/psum | solution.py:92
  421.9 1.8 broadcast_divide_fusion
  (28 shorter events, 0.6 us)
Async XLA Ops:
  7.2 131.8 %copy-start = (bf16[1,480,2304]{2,1,0:T(8,128)(2,1)S(1)}, bf16[1,480,2304]{2,1,0:T(8,128)(2,1)}, u32[]{:S(2)}) copy-start(bf16[1,480,2304]{2,1,0:T(8,128)(2,1)} %param.13) | copy-start | bytes 6635524
  7.2 112.3 %all-gather.3.cloned.1.call-start = ((), (), s32[]{:S(2)}) async-start(), calls=%async_computation.5 | async-start | bytes 15925248 | tf_op jit(solution)/shard_map/all_gather | solution.py:66
  46.3 182.4 %reduce-scatter.2.cloned.1.call-start = ((), (), s32[]{:S(2)}) async-start(), calls=%async_computation.3 | async-start | bytes 15925248 | tf_op jit(solution)/shard_map/reduce_scatter | solution.py:68
  119.5 11.4 %copy-start.5 = (bf16[128,24,2304]{2,0,1:T(8,128)(2,1)S(1)}, bf16[128,24,2304]{2,0,1:T(8,128)(2,1)}, u32[]{:S(2)}) copy-start(bf16[128,24,2304]{2,0,1:T(8,128)(2,1)} %all-gather.3.cloned.1.call-done) | copy-start | bytes 42467332
  119.5 11.4 %copy-start.6 = (bf16[1,2304,480]{1,2,0:T(8,128)(2,1)S(1)}, bf16[1,2304,480]{1,2,0:T(8,128)(2,1)}, u32[]{:S(2)}) copy-start(bf16[1,2304,480]{1,2,0:T(8,128)(2,1)} %param.11) | copy-start | bytes 6635524
  232.0 7.1 %copy-start.2 = (s32[64,2]{0,1:T(2,128)S(1)}, s32[64,2]{0,1:T(2,128)}, u32[]{:S(2)}) copy-start(s32[64,2]{0,1:T(2,128)} %param.8) | copy-start | bytes 1540
  232.0 7.5 %copy-start.3 = (f32[64,2]{0,1:T(2,128)S(1)}, f32[64,2]{0,1:T(2,128)}, u32[]{:S(2)}) copy-start(f32[64,2]{0,1:T(2,128)} %param.9) | copy-start | bytes 1540
  232.0 30.9 %all-to-all-start.1 = ((bf16[16,1,24,2304]{3,2,1,0:T(8,128)(2,1)}), bf16[16,1,24,2304]{3,2,1,0:T(8,128)(2,1)}, u32[]{:S(2)}, u32[]{:S(2)}) async-start(bf16[16,1,24,2304]{3,2,1,0:T(8,128)(2,1)} %copy.37), calls=%async_computation.2 | async-start | bytes 3538944 | tf_op jit(solution)/shard_map/all_to_all | solution.py:76
  238.9 183.0 %all-reduce.2.cloned.1.call-start = ((), (), s32[]{:S(2)}) async-start(), calls=%async_computation.4 | async-start | bytes 589824 | tf_op jit(solution)/shard_map/psum | solution.py:92
  270.0 6.3 %copy-start.4 = (s32[64]{0:T(128)S(1)}, s32[64]{0:T(128)}, u32[]{:S(2)}) copy-start(s32[64]{0:T(128)} %param.10) | copy-start | bytes 772
  276.3 147.3 %copy-start.1 = (bf16[64,2304]{1,0:T(8,128)(2,1)}, bf16[64,2304]{1,0:T(8,128)(2,1)S(1)}, u32[]{:S(2)}) copy-start(bf16[64,2304]{1,0:T(8,128)(2,1)S(1)} %fusion.11) | copy-start | bytes 884740
Sparse Core Ops, SparseCore 0:
  46.5 72.9 all-gather.2
  149.4 79.3 reduce-scatter.1
  277.4 144.4 all-reduce.1
where the time goes:
time: 431 us; the launch traced here: 430 us
  waiting for transfers between devices  252 us (58%)
  blocking collectives  101 us (23%)
  matrix products  32 us (7%)
  between operations  13.9 us (3%)
  local copies, waits for them, and re-layouts  12.5 us (3%)
  other arithmetic  11.7 us (3%)
  starting transfers between devices  7.18 us (2%)
    reduce_scatter x1, waiting for transfers between devices, shards(): lax.psum_scatter(jnp.einsum('nacf,afd->nacd', hidden, w_down, preferred_e...  79.5 us
    psum x1, waiting for transfers between devices, shards(): lax.psum((seq_sums, seq_counts), ('dp', 'tensor', 'expert'))  75.9 us
    all_gather x1, waiting for transfers between devices, shards(): lax.all_gather(local_rows, ('dp', 'tensor'), axis=0, tiled=True)  73.1 us
    psum x1, blocking collectives, shards(): lax.psum((seq_sums, seq_counts), ('dp', 'tensor', 'expert'))  68.6 us
    all_to_all x1, blocking collectives, shards(): lax.all_to_all(send_rows, 'expert', split_axis=0, concat_axis=0, tiled=True)  32.4 us
    all_to_all x1, waiting for transfers between devices, shards(): lax.all_to_all(summed, 'expert', split_axis=0, concat_axis=0, tiled=True)  23.3 us
    dot_general x1, matrix products, expert_hidden(): jnp.einsum('nacd,adf->nacf', row_block, w_up, preferred_element_type=jnp....  11.4 us
    dot_general x1, matrix products, shards(): jnp.einsum('nacf,afd->nacd', hidden, w_down, preferred_element_type=jnp.f...  10.3 us
  transfers between devices with their start and end apart: 4, of which 4 were waited for; matrix products, arithmetic and copies ran while one was open for 0% of the time, Pallas kernels for 0%

commit v1 on v0

v1 whole, which is shorter than its diff:
```python
import jax
import jax.numpy as jnp
from jax import lax
from jax.experimental import pallas as pl
from jax.experimental.pallas import tpu as pltpu
from jax.sharding import PartitionSpec as P

EXPERTS = 8
TOP = 2
CAP = 24
epsilon = 1e-06

NX = 4
NY = 4
NZ = 4
PLANE = NY * NZ
D = 2304
FFD = 480
FFC = 1024
TOK = 64
NSEQ = 32
ROWS = PLANE * CAP
PW = D + 128
MESH = pl.DeviceIdType.MESH
bf16 = jnp.bfloat16
f32 = jnp.float32


def place():
    expert = lax.axis_index("expert")
    return lax.axis_index("dp"), lax.axis_index("tensor"), expert // NY, expert % NY


def moved(dx=0, dc=0, dz=0, dy=0):
    x, c, z, y = place()
    return ((x + dx) % NX, (c + dc) % 2, ((z + dz) % NZ) * NY + (y + dy) % NY)


def dot(a, b, dims=((1,), (0,))):
    return lax.dot_general(a, b, (dims, ((), ())), preferred_element_type=f32)


def kernel(
    tok_ref, routes_ref, gates_ref, seg_ref, wg_ref, wu_ref, wd_ref, emb_ref, pool_ref,
    sbuf, wbuf, rbuf, hbuf, tbuf, vbuf, qbuf, ubuf, ret, pb, pr, p2, p2r, p3,
    w_ls, w_ss, w_rs, d_ss, d_rs, l_s, x_ss, x_rs, y_ss, y_rs, b_ss, b_rs, p_ss, p_rs, p2_ss, p2_rs, p3_ss, p3_rs,
):
    x, c, z, y = place()
    me = lax.axis_index("expert")
    plane = [(dz, dy) for dz in range(NZ) for dy in range(NY) if dz or dy]
    line = [(dx, dc) for dx in range(NX) for dc in range(2) if dx or dc]

    def remote(src, dst, send, recv, target):
        return pltpu.make_async_remote_copy(
            src_ref=src, dst_ref=dst, send_sem=send, recv_sem=recv, device_id=target, device_id_type=MESH
        )

    barrier = pltpu.get_barrier_semaphore()
    for dz, dy in plane:
        pl.semaphore_signal(barrier, inc=1, device_id=moved(0, 0, dz, dy), device_id_type=MESH)
    for dx, dc in line:
        pl.semaphore_signal(barrier, inc=1, device_id=moved(dx, dc), device_id_type=MESH)

    weights = (wg_ref, wu_ref, wd_ref)
    loads = [pltpu.make_async_copy(w, wbuf.at[k, pl.ds(0, FFD)], w_ls.at[k]) for k, w in enumerate(weights)]
    for copy in loads:
        copy.start()

    both = jnp.concatenate(
        [routes_ref[...].astype(f32), gates_ref[...], jnp.zeros((4, TOK), f32)], axis=0
    )
    both = jnp.concatenate([both, jnp.zeros((8, 128 - TOK), f32)], axis=1)
    columns = both.T[:TOK]
    r0, r1 = routes_ref[0:1, :], routes_ref[1:2, :]
    experts = lax.broadcasted_iota(jnp.int32, (EXPERTS, TOK), 0)
    named = jnp.where((experts == r0) | (experts == r1), 1.0, 0.0)
    earlier = lax.broadcasted_iota(jnp.int32, (TOK, TOK), 0) < lax.broadcasted_iota(jnp.int32, (TOK, TOK), 1)
    rank = dot(named.astype(bf16), jnp.where(earlier, 1.0, 0.0).astype(bf16))
    spot = jnp.where(named > 0.5, rank, -1.0)
    slots = lax.broadcasted_iota(jnp.int32, (EXPERTS, CAP, TOK), 1).astype(f32)
    place_rows = jnp.where(slots == spot[:, None, :], 1.0, 0.0).reshape(EXPERTS * CAP, TOK).astype(bf16)

    values = tok_ref[...].astype(f32)
    scale = lax.rsqrt(jnp.mean(values * values, axis=1, keepdims=True) + epsilon)
    normed = (values * scale).astype(bf16)
    sbuf[...] = dot(place_rows, normed).astype(bf16).reshape(EXPERTS, CAP, D)
    wbuf[:, pl.ds(2 * FFD, FFC - 2 * FFD), :] = jnp.zeros((3, FFC - 2 * FFD, D), bf16)

    pl.semaphore_wait(barrier, len(plane) + len(line))

    sends = []
    own = pltpu.make_async_copy(sbuf.at[me // 2], rbuf.at[0, 0], l_s.at[0])
    own.start()
    for dz, dy in plane:
        target = moved(0, 0, dz, dy)
        back = ((NZ - dz) % NZ) * NY + (NY - dy) % NY
        copy = remote(sbuf.at[target[2] // 2], rbuf.at[0, back], d_ss.at[back], d_rs.at[back], target)
        copy.start()
        sends.append(copy)
    pair = [
        remote(w, wbuf.at[k, pl.ds(FFD, FFD)], w_ss.at[k], w_rs.at[k], moved(0, 1))
        for k, w in enumerate(weights)
    ]
    for copy in pair:
        copy.start()

    def group(d, g):
        return rbuf.at[d, pl.ds(g * NY, NY)]

    own.wait()
    for g in range(NZ):
        for i in range(g * NY, (g + 1) * NY):
            if i:
                remote(sbuf.at[0], rbuf.at[0, i], d_ss.at[i], d_rs.at[i], moved()).wait_recv()
        for dx, d in ((1, 3), (3, 1)):
            copy = remote(group(0, g), group(d, g), x_ss.at[d, g], x_rs.at[d, g], moved(dx))
            copy.start()
            sends.append(copy)

    def arrived(d, g):
        remote(group(0, g), group(d, g), x_ss.at[d, g], x_rs.at[d, g], moved(1)).wait_recv()

    def ffn(d):
        @pl.loop(0, FFC // 256)
        def _(j):
            part = pl.ds(pl.multiple_of(j * 256, 256), 256)
            rows = rbuf[d].reshape(ROWS, D)
            gate = dot(rows, wbuf[0, part, :], ((1,), (1,)))
            up = dot(rows, wbuf[1, part, :], ((1,), (1,)))
            hbuf[:, part] = (gate / (1.0 + jnp.exp(-gate)) * up).astype(bf16)

        @pl.loop(0, D // 768)
        def _(j):
            part = pl.ds(pl.multiple_of(j * 768, 256), 768)
            tbuf[d, :, :, part] = dot(hbuf[...], wbuf[2, :, part]).astype(bf16).reshape(PLANE, CAP, 768)

    for copy in loads:
        copy.wait()
    for copy in pair:
        copy.wait()
    ffn(0)
    for k in range(2):
        for d, g, dx in ((3, k, 1), (1, k + 2, 3)):
            arrived(d, g)
            copy = remote(group(d, g), group(2, g), x_ss.at[2, g], x_rs.at[2, g], moved(dx))
            copy.start()
            sends.append(copy)
    for g in (2, 3):
        arrived(3, g)
    ffn(3)

    def half(ref, k):
        return ref.at[pl.ds(k * 8, 8)]

    def give(src, dst, k, dx):
        copy = remote(src, dst, y_ss.at[k], y_rs.at[k], moved(dx))
        copy.start()
        sends.append(copy)

    def taken(dst, k):
        remote(dst, dst, y_ss.at[k], y_rs.at[k], moved(1)).wait_recv()

    give(half(tbuf.at[3], 0), half(vbuf.at[1], 0), 0, 3)
    for g in (0, 1):
        arrived(1, g)
    ffn(1)
    give(half(tbuf.at[1], 1), half(vbuf.at[0], 1), 1, 1)
    for g in range(NZ):
        arrived(2, g)
    ffn(2)
    give(half(tbuf.at[2], 0), qbuf.at[0], 2, 1)
    give(half(tbuf.at[2], 1), qbuf.at[1], 3, 3)

    def add(d, k, q):
        @pl.loop(k * 8, k * 8 + 8)
        def _(i):
            tbuf[d, i] = (tbuf[d, i].astype(f32) + qbuf[q, i - k * 8].astype(f32)).astype(bf16)

    taken(qbuf.at[0], 2)
    add(1, 0, 0)
    give(half(tbuf.at[1], 0), half(vbuf.at[0], 0), 4, 1)
    taken(qbuf.at[1], 3)
    add(3, 1, 1)
    give(half(tbuf.at[3], 1), half(vbuf.at[1], 1), 5, 3)

    taken(half(vbuf.at[1], 0), 0)
    taken(half(vbuf.at[0], 1), 1)
    for k in range(2):
        if k == 0:
            taken(half(vbuf.at[0], 0), 4)
        else:
            taken(half(vbuf.at[1], 1), 5)

        @pl.loop(k * 8, k * 8 + 8)
        def _(i):
            ubuf[i] = (tbuf[0, i].astype(f32) + vbuf[0, i].astype(f32) + vbuf[1, i].astype(f32)).astype(bf16)

        for i in range(k * 8, k * 8 + 8):
            if i:
                target = moved(0, 0, i // NY, i % NY)
                copy = remote(ubuf.at[i], ret.at[me], b_ss.at[i], b_rs.at[me], target)
                copy.start()
                sends.append(copy)
    ret[me] = ubuf[0]

    lanes = lax.broadcasted_iota(jnp.int32, (TOK, 2 * EXPERTS * CAP), 1).astype(f32)
    eights = lax.broadcasted_iota(jnp.int32, (TOK, EXPERTS), 1).astype(f32)
    later = lax.broadcasted_iota(jnp.int32, (TOK, TOK), 0) > lax.broadcasted_iota(jnp.int32, (TOK, TOK), 1)
    q0, q1 = columns[:, 0:1], columns[:, 1:2]
    names = jnp.where((eights == q0) | (eights == q1), 1.0, 0.0)
    ranks = dot(jnp.where(later, 1.0, 0.0).astype(bf16), names.astype(bf16))
    mix = jnp.zeros((TOK, 2 * EXPERTS * CAP), f32)
    for q, gate in ((q0, columns[:, 2:3]), (q1, columns[:, 3:4])):
        at = q * (2 * CAP) + jnp.sum(jnp.where(eights == q, ranks, 0.0), axis=1, keepdims=True)
        mix = mix + jnp.where((lanes == at) | (lanes == at + CAP), gate, 0.0)
    high = mix.astype(bf16)
    low = (mix - high.astype(f32)).astype(bf16)

    for dz, dy in plane:
        target = moved(0, 0, dz, dy)
        remote(ubuf.at[0], ret.at[target[2]], b_ss.at[0], b_rs.at[target[2]], target).wait_recv()
    hot = (lax.broadcasted_iota(jnp.int32, (NSEQ, TOK), 0) == seg_ref[...]).astype(f32)
    count = jnp.broadcast_to(jnp.sum(hot, axis=1, keepdims=True), (NSEQ, 128))
    hot = hot.astype(bf16)

    @pl.loop(0, D // 768)
    def _(j):
        part = pl.ds(pl.multiple_of(j * 768, 256), 768)
        rows = ret[:, :, part].reshape(ROWS, 768)
        mixed = tok_ref[:, part].astype(f32) + (dot(high, rows) + dot(low, rows))
        embedded = mixed.astype(bf16)
        emb_ref[:, part] = embedded
        sums = dot(hot, embedded)
        for i in range(PLANE):
            pb[i, :, part] = sums[2 * i : 2 * i + 2]

    for i in range(PLANE):
        pb[i, :, D:] = count[2 * i : 2 * i + 2]

    for dz, dy in plane:
        target = moved(0, 0, dz, dy)
        copy = remote(pb.at[target[2]], pr.at[me], p_ss.at[target[2]], p_rs.at[me], target)
        copy.start()
        sends.append(copy)
    pr[me] = pb[me]
    for dz, dy in plane:
        target = moved(0, 0, dz, dy)
        remote(pb.at[0], pr.at[target[2]], p_ss.at[0], p_rs.at[target[2]], target).wait_recv()
    p2[...] = jnp.sum(pr[...], axis=0)
    mine = x * 2 + c
    for k, (dx, dc) in enumerate(line):
        target = moved(dx, dc)
        copy = remote(p2, p2r.at[mine], p2_ss.at[k], p2_rs.at[mine], target)
        copy.start()
        sends.append(copy)
    p2r[mine] = p2[...]
    for k, (dx, dc) in enumerate(line):
        target = moved(dx, dc)
        other = target[0] * 2 + target[1]
        remote(p2, p2r.at[other], p2_ss.at[k], p2_rs.at[other], target).wait_recv()
    total = jnp.sum(p2r[...], axis=0)
    p3[me] = total[:, :D] / jnp.concatenate([total[:, D:]] * (D // 128), axis=1)
    for dz, dy in plane:
        target = moved(0, 0, dz, dy)
        copy = remote(p3.at[me], p3.at[me], p3_ss.at[target[2]], p3_rs.at[me], target)
        copy.start()
        sends.append(copy)
    for dz, dy in plane:
        target = moved(0, 0, dz, dy)
        remote(p3.at[target[2]], p3.at[target[2]], p3_ss.at[0], p3_rs.at[target[2]], target).wait_recv()
    for i in range(PLANE):
        pool_ref[2 * i : 2 * i + 2, :] = p3[i]
    for copy in sends:
        copy.wait_send()


def shards(tokens, routes, gates, segments, w_gate, w_up, w_down):
    vmem = pl.BlockSpec(memory_space=pltpu.VMEM)
    hbm = pl.BlockSpec(memory_space=pl.ANY)
    sem = pltpu.SemaphoreType.DMA
    return pl.pallas_call(
        kernel,
        name="moe",
        out_shape=(
            jax.ShapeDtypeStruct((TOK, D), bf16),
            jax.ShapeDtypeStruct((NSEQ, D), f32),
        ),
        in_specs=[vmem] * 4 + [hbm] * 3,
        out_specs=(vmem, vmem),
        scratch_shapes=[
            pltpu.VMEM((EXPERTS, CAP, D), bf16),
            pltpu.VMEM((3, FFC, D), bf16),
            pltpu.VMEM((NX, PLANE, CAP, D), bf16),
            pltpu.VMEM((ROWS, FFC), bf16),
            pltpu.VMEM((NX, PLANE, CAP, D), bf16),
            pltpu.VMEM((2, PLANE, CAP, D), bf16),
            pltpu.VMEM((2, PLANE // 2, CAP, D), bf16),
            pltpu.VMEM((PLANE, CAP, D), bf16),
            pltpu.VMEM((PLANE, CAP, D), bf16),
            pltpu.VMEM((PLANE, 2, PW), f32),
            pltpu.VMEM((PLANE, 2, PW), f32),
            pltpu.VMEM((2, PW), f32),
            pltpu.VMEM((8, 2, PW), f32),
            pltpu.VMEM((PLANE, 2, D), f32),
            sem((3,)), sem((3,)), sem((3,)),
            sem((PLANE,)), sem((PLANE,)), sem((1,)),
            sem((NX, NZ)), sem((NX, NZ)),
            sem((6,)), sem((6,)),
            sem((PLANE,)), sem((PLANE,)),
            sem((PLANE,)), sem((PLANE,)),
            sem((8,)), sem((8,)),
            sem((PLANE,)), sem((PLANE,)),
        ],
        compiler_params=pltpu.CompilerParams(
            collective_id=0, has_side_effects=True, vmem_limit_bytes=58 * 2**20
        ),
    )(
        tokens,
        routes.T,
        gates.T,
        segments[None, :],
        jnp.swapaxes(w_gate[0], 0, 1),
        jnp.swapaxes(w_up[0], 0, 1),
        w_down[0],
    )


def solution(mesh):
    placed = (
        P(("dp", "tensor", "expert"), None),
        P(("dp", "tensor", "expert"), None),
        P(("dp", "tensor", "expert"), None),
        P(("dp", "tensor", "expert")),
        P("expert", None, ("dp", "tensor")),
        P("expert", None, ("dp", "tensor")),
        P("expert", ("dp", "tensor"), None),
    )
    return jax.shard_map(
        shards,
        mesh=mesh,
        in_specs=placed,
        out_specs=(P(("dp", "tensor", "expert"), None), P()),
        check_vma=False,
    )
```

time: 431 us -> 193 us (0.45)
  waiting for transfers between devices: 252 us -> 0 us
  Pallas kernels: 0 us -> 189 us
  blocking collectives: 101 us -> 0 us
  matrix products: 32 us -> 0 us
  between operations: 13.9 us -> 0.64 us
  other arithmetic: 11.7 us -> 0 us
  local copies, waits for them, and re-layouts: 12.5 us -> 3.39 us
  starting transfers between devices: 7.18 us -> 0 us
    pallas_call x0 -> x1, Pallas kernels: none -> 189 us  [shards(): pl.pallas_call(kernel, name='moe', out_shape=(jax.ShapeDtypeStruct((TOK,...]
    reduce_scatter x1 -> x0, waiting for transfers between devices: 79.5 us -> none  [shards(): lax.psum_scatter(jnp.einsum('nacf,afd->nacd', hidden, w_down, preferred_e...]
    psum x1 -> x0, waiting for transfers between devices: 75.9 us -> none  [shards(): lax.psum((seq_sums, seq_counts), ('dp', 'tensor', 'expert'))]
    all_gather x1 -> x0, waiting for transfers between devices: 73.1 us -> none  [shards(): lax.all_gather(local_rows, ('dp', 'tensor'), axis=0, tiled=True)]
    psum x1 -> x0, blocking collectives: 68.6 us -> none  [shards(): lax.psum((seq_sums, seq_counts), ('dp', 'tensor', 'expert'))]
    all_to_all x1 -> x0, blocking collectives: 32.4 us -> none  [shards(): lax.all_to_all(send_rows, 'expert', split_axis=0, concat_axis=0, tiled=True)]
    dot_general x5 -> x0, matrix products: 32 us -> none  [the longest x1 11.4 us: expert_hidden(): jnp.einsum('nacd,adf->nacf', row_block, w_up, preferred_element_type=jnp....]
    all_to_all x1 -> x0, waiting for transfers between devices: 23.3 us -> none  [shards(): lax.all_to_all(summed, 'expert', split_axis=0, concat_axis=0, tiled=True)]
  transfers between devices with their start and end apart: 4 -> 0, of which waited for: 4 -> 0; matrix products, arithmetic and copies ran while one was open for 0% -> 0% of each run, Pallas kernels for 0% -> 0%
where the time goes in v1:
time: 193 us
  Pallas kernels  189 us (98%)
  local copies, waits for them, and re-layouts  3.39 us (2%)
    pallas_call x1, Pallas kernels, shards(): pl.pallas_call(kernel, name='moe', out_shape=(jax.ShapeDtypeStruct((TOK,...  189 us

profile of v1, /device:TPU:1, one launch (start us, length us, event | category | flops | bytes accessed | tf_op | source)
XLA Modules:
  0.0 192.7 jit_solution(16670364747486085612)
XLA Ops:
  0.6 188.6 %moe.1 = (bf16[64,2304]{1,0:T(8,128)(2,1)}, f32[32,2304]{1,0:T(8,128)}) custom-call(bf16[64,2304]{1,0:T(8,128)(2,1)} %tok_ref.1, s32[2,64]{1,0:T(2,128)} %bitcast.13, f32[2,64]{1,0:T(2,128)} %bitcast.14, s32[1,64]{1,0:T(1,128)} %bitcast.15, bf16[480,2304]{1,0:T(8,128)(2,1)} %bitcast.10, bf16[480,2304]{1,0:T(8,128)(2,1)} %bitcast.11, bf16[480,2304]{1,0:T(8,128)(2,1)} %bitcast.12), custom_call_target="tpu_custom_call" | custom-call | tf_op jit(solution)/shard_map/moe/pallas_call | solution.py:281
  189.3 1.7 copy.11
  191.0 1.7 copy.12

commit v2 on v1

v2 whole, which is shorter than its diff:
```python
import jax
import jax.numpy as jnp
from jax import lax
from jax.experimental import pallas as pl
from jax.experimental.pallas import tpu as pltpu
from jax.sharding import PartitionSpec as P

EXPERTS = 8
TOP = 2
CAP = 24
epsilon = 1e-06

NX = 4
NY = 4
NZ = 4
PLANE = NY * NZ
D = 2304
FFD = 480
FFC = 1024
TOK = 64
NSEQ = 32
ROWS = PLANE * CAP
CB = 768
CA = D - CB
PW = D + 128
MESH = pl.DeviceIdType.MESH
bf16 = jnp.bfloat16
f32 = jnp.float32


def place():
    expert = lax.axis_index("expert")
    return lax.axis_index("dp"), lax.axis_index("tensor"), expert // NY, expert % NY


def moved(dx=0, dc=0, dz=0, dy=0):
    x, c, z, y = place()
    return ((x + dx) % NX, (c + dc) % 2, ((z + dz) % NZ) * NY + (y + dy) % NY)


def dot(a, b, dims=((1,), (0,))):
    return lax.dot_general(a, b, (dims, ((), ())), preferred_element_type=f32)


def kernel(
    tok_ref, routes_ref, gates_ref, seg_ref, wg_ref, wu_ref, wd_ref, emb_ref, pool_ref,
    sa, sb, wbuf, ra, rb, hbuf, ta, tb, va, qa, ua, reta, retb, raw, meta, mixed, pb, pr, p2, p2r, p3,
    w_ls, w_ss, w_rs, l_s, raw_ss, raw_rs, meta_ss, meta_rs, da_ss, da_rs, db_ss, db_rs, x_ss, x_rs, x2_ss, x2_rs,
    y_ss, y_rs, ba_ss, ba_rs, bb_ss, bb_rs, m_ss, m_rs, p_ss, p_rs, p2_ss, p2_rs, p3_ss, p3_rs,
):
    x, c, z, y = place()
    me = lax.axis_index("expert")
    plane = [(dz, dy) for dz in (0, 3, 2, 1) for dy in range(NY) if dz or dy]
    line = [(dx, dc) for dx in range(NX) for dc in range(2) if dx or dc]
    around = (1, 3, 2)
    sends = []

    def remote(src, dst, send, recv, target):
        return pltpu.make_async_remote_copy(
            src_ref=src, dst_ref=dst, send_sem=send, recv_sem=recv, device_id=target, device_id_type=MESH
        )

    def give(src, dst, send, recv, target):
        copy = remote(src, dst, send, recv, target)
        copy.start()
        sends.append(copy)

    def taken(dst, recv):
        remote(dst, dst, recv, recv, moved(1)).wait_recv()

    barrier = pltpu.get_barrier_semaphore()
    for dz, dy in plane:
        pl.semaphore_signal(barrier, inc=1, device_id=moved(0, 0, dz, dy), device_id_type=MESH)
    for dx, dc in line:
        pl.semaphore_signal(barrier, inc=1, device_id=moved(dx, dc), device_id_type=MESH)

    weights = (wg_ref, wu_ref, wd_ref)
    loads = [pltpu.make_async_copy(w, wbuf.at[k, pl.ds(0, FFD)], w_ls.at[k]) for k, w in enumerate(weights)]
    for copy in loads:
        copy.start()

    meta[0] = jnp.concatenate(
        [
            jnp.concatenate([routes_ref[...].astype(f32), gates_ref[...], jnp.zeros((4, TOK), f32)], axis=0),
            jnp.zeros((8, 128 - TOK), f32),
        ],
        axis=1,
    )
    experts = lax.broadcasted_iota(jnp.int32, (EXPERTS, TOK), 0).astype(f32)
    earlier = lax.broadcasted_iota(jnp.int32, (TOK, TOK), 0) < lax.broadcasted_iota(jnp.int32, (TOK, TOK), 1)
    earlier = jnp.where(earlier, 1.0, 0.0).astype(bf16)
    slots = lax.broadcasted_iota(jnp.int32, (EXPERTS, CAP, TOK), 1).astype(f32)

    def place_rows(d):
        rows = meta[d]
        named = jnp.where((experts == rows[0:1, :TOK]) | (experts == rows[1:2, :TOK]), 1.0, 0.0)
        spot = jnp.where(named > 0.5, dot(named.astype(bf16), earlier), -1.0)
        return jnp.where(slots == spot[:, None, :], 1.0, 0.0).reshape(EXPERTS * CAP, TOK).astype(bf16)

    values = tok_ref[...].astype(f32)
    scale = lax.rsqrt(jnp.mean(values * values, axis=1, keepdims=True) + epsilon)
    normed = (values * scale).astype(bf16)
    raw[0] = normed[:, CA:]

    pl.semaphore_wait(barrier, len(plane) + len(line))
    for dx in around:
        d = (NX - dx) % NX
        give(meta.at[0], meta.at[d], meta_ss.at[d], meta_rs.at[d], moved(dx))
        give(raw.at[0], raw.at[d], raw_ss.at[d], raw_rs.at[d], moved(dx))
    spots = place_rows(0)
    sa[...] = dot(spots, normed[:, :CA]).astype(bf16).reshape(EXPERTS, CAP, CA)
    own = [pltpu.make_async_copy(sa.at[me // 2], ra.at[0, 0], l_s.at[0])]
    own[0].start()
    for dz, dy in plane:
        target = moved(0, 0, dz, dy)
        back = ((NZ - dz) % NZ) * NY + (NY - dy) % NY
        give(sa.at[target[2] // 2], ra.at[back, 0], da_ss.at[back], da_rs.at[back], target)
    for k, w in enumerate(weights):
        give(w, wbuf.at[k, pl.ds(FFD, FFD)], w_ss.at[k], w_rs.at[k], moved(0, 1))
    sb[:, 0] = dot(spots, raw[0]).astype(bf16).reshape(EXPERTS, CAP, CB)
    for d in around:
        taken(meta.at[d], meta_rs.at[d])
        taken(raw.at[d], raw_rs.at[d])
        sb[:, d] = dot(place_rows(d), raw[d]).astype(bf16).reshape(EXPERTS, CAP, CB)
    own.append(pltpu.make_async_copy(sb.at[me // 2], rb.at[0], l_s.at[1]))
    own[1].start()
    for dz, dy in plane:
        target = moved(0, 0, dz, dy)
        back = ((NZ - dz) % NZ) * NY + (NY - dy) % NY
        give(sb.at[target[2] // 2], rb.at[back], db_ss.at[back], db_rs.at[back], target)
    wbuf[:, pl.ds(2 * FFD, FFC - 2 * FFD), :] = jnp.zeros((3, FFC - 2 * FFD, D), bf16)

    def four(g):
        return pl.ds(g * NY, NY)

    def two(g, k):
        return pl.ds(g * NY + 2 * k, 2)

    def forward(g):
        for i in range(g * NY, (g + 1) * NY):
            if i:
                taken(ra.at[i, 0], da_rs.at[i])
            else:
                own[0].wait()
        for dx, d in ((1, 3), (3, 1)):
            give(ra.at[four(g), 0], ra.at[four(g), d], x_ss.at[d, g], x_rs.at[d, g], moved(dx))

    def relay(g):
        for k, d, dx in ((0, 3, 1), (1, 1, 3)):
            taken(ra.at[four(g), d], x_rs.at[d, g])
            give(ra.at[two(g, k), d], ra.at[two(g, k), 2], x2_ss.at[k, g], x2_rs.at[k, g], moved(dx))

    def ffn(g):
        for k in range(2):
            taken(ra.at[two(g, k), 2], x2_rs.at[k, g])
        for i in range(g * NY, (g + 1) * NY):
            if i:
                taken(rb.at[i], db_rs.at[i])
            else:
                own[1].wait()

        @pl.loop(0, FFC // 256)
        def _(j):
            part = pl.ds(pl.multiple_of(j * 256, 256), 256)
            rows_a = ra[g * NY : (g + 1) * NY].reshape(ROWS, CA)
            rows_b = rb[g * NY : (g + 1) * NY].reshape(ROWS, CB)
            nt = ((1,), (1,))
            gate = dot(rows_a, wbuf[0, part, :CA], nt) + dot(rows_b, wbuf[0, part, CA:], nt)
            up = dot(rows_a, wbuf[1, part, :CA], nt) + dot(rows_b, wbuf[1, part, CA:], nt)
            hbuf[:, part] = (gate / (1.0 + jnp.exp(-gate)) * up).astype(bf16)

        for ref, first, width in ((tb, CA, CB), (ta, 0, CA)):
            @pl.loop(0, width // 768)
            def _(j):
                part = pl.ds(pl.multiple_of(j * 768, 256), 768)
                down = pl.ds(pl.multiple_of(first + j * 768, 256), 768)
                ref[g * NY : (g + 1) * NY, :, :, part] = (
                    dot(hbuf[...], wbuf[2, :, down]).astype(bf16).reshape(NY, NX, CAP, 768)
                )

    def sums(g):
        for k, dx in ((0, 1), (1, 3)):
            give(ta.at[two(g, k), 2], qa.at[k, pl.ds(2 * g, 2)], y_ss.at[0, k, g], y_rs.at[0, k, g], moved(dx))
        for k, d, v in ((1, 1, 0), (0, 3, 1)):
            give(ta.at[two(g, k), d], va.at[v, two(g, k)], y_ss.at[1, v, g], y_rs.at[1, v, g], moved(d))
        for i in range(g * NY, (g + 1) * NY):
            if i:
                give(tb.at[i], retb.at[me], bb_ss.at[i], bb_rs.at[me], moved(0, 0, i // NY, i % NY))
            else:
                retb[me] = tb[0]

    def pass_on(g):
        for k, d, v in ((0, 1, 0), (1, 3, 1)):
            taken(qa.at[k, pl.ds(2 * g, 2)], y_rs.at[0, k, g])
            for i in range(2):
                at = g * NY + 2 * k + i
                ta[at, d] = (ta[at, d].astype(f32) + qa[k, 2 * g + i].astype(f32)).astype(bf16)
            give(ta.at[two(g, k), d], va.at[v, two(g, k)], y_ss.at[2, v, g], y_rs.at[2, v, g], moved(d))

    def finish(g):
        for k, v in ((1, 0), (0, 1)):
            taken(va.at[v, two(g, k)], y_rs.at[1, v, g])
        for k, v in ((0, 0), (1, 1)):
            taken(va.at[v, two(g, k)], y_rs.at[2, v, g])
        for i in range(g * NY, (g + 1) * NY):
            total = (ta[i, 0].astype(f32) + va[0, i].astype(f32) + va[1, i].astype(f32)).astype(bf16)
            if i:
                ua[i] = total
                give(ua.at[i], reta.at[me], ba_ss.at[i], ba_rs.at[me], moved(0, 0, i // NY, i % NY))
            else:
                reta[me] = total

    forward(0)
    forward(1)
    relay(0)
    forward(2)
    relay(1)
    forward(3)
    relay(2)
    for copy in loads:
        copy.wait()
    for k in range(3):
        taken(wbuf.at[k, pl.ds(FFD, FFD)], w_rs.at[k])
    ffn(0)
    sums(0)
    relay(3)
    ffn(1)
    sums(1)
    pass_on(0)
    ffn(2)
    sums(2)
    pass_on(1)
    finish(0)
    ffn(3)
    sums(3)
    pass_on(2)
    finish(1)

    lanes = lax.broadcasted_iota(jnp.int32, (TOK, 2 * EXPERTS * CAP), 1).astype(f32)
    eights = lax.broadcasted_iota(jnp.int32, (TOK, EXPERTS), 1).astype(f32)
    later = lax.broadcasted_iota(jnp.int32, (TOK, TOK), 0) > lax.broadcasted_iota(jnp.int32, (TOK, TOK), 1)
    later = jnp.where(later, 1.0, 0.0).astype(bf16)

    def gate_rows(d):
        columns = jnp.concatenate([meta[d], jnp.zeros((120, 128), f32)], axis=0).T[:TOK]
        q0, q1 = columns[:, 0:1], columns[:, 1:2]
        names = jnp.where((eights == q0) | (eights == q1), 1.0, 0.0)
        ranks = dot(later, names.astype(bf16))
        mix = jnp.zeros((TOK, 2 * EXPERTS * CAP), f32)
        for q, gate in ((q0, columns[:, 2:3]), (q1, columns[:, 3:4])):
            at = q * (2 * CAP) + jnp.sum(jnp.where(eights == q, ranks, 0.0), axis=1, keepdims=True)
            mix = mix + jnp.where((lanes == at) | (lanes == at + CAP), gate, 0.0)
        high = mix.astype(bf16)
        return high, (mix - high.astype(f32)).astype(bf16)

    def mixture(gate, rows):
        return dot(gate[0], rows) + dot(gate[1], rows)

    gates = [gate_rows(d) for d in range(NX)]
    pass_on(3)
    finish(2)
    for dz, dy in plane:
        other = moved(0, 0, dz, dy)[2]
        taken(retb.at[other], bb_rs.at[other])
    for d in around:
        mixed[d, 0] = mixture(gates[d], retb[:, d].reshape(ROWS, CB)).astype(bf16)
        give(mixed.at[d, 0], mixed.at[(NX - d) % NX, 1], m_ss.at[d], m_rs.at[(NX - d) % NX], moved(d))
    finish(3)
    own_mix = mixture(gates[0], retb[:, 0].reshape(ROWS, CB))

    hot = (lax.broadcasted_iota(jnp.int32, (NSEQ, TOK), 0) == seg_ref[...]).astype(f32)
    count = jnp.broadcast_to(jnp.sum(hot, axis=1, keepdims=True), (NSEQ, 128))
    hot = hot.astype(bf16)

    def pool(embedded, part):
        emb_ref[:, part] = embedded
        sums = dot(hot, embedded)
        for i in range(PLANE):
            pb[i, :, part] = sums[2 * i : 2 * i + 2]

    for d in around:
        taken(mixed.at[d, 1], m_rs.at[d])
        own_mix = own_mix + mixed[d, 1].astype(f32)
    pool((tok_ref[:, CA:].astype(f32) + own_mix).astype(bf16), pl.ds(CA, CB))
    for dz, dy in plane:
        other = moved(0, 0, dz, dy)[2]
        taken(reta.at[other], ba_rs.at[other])

    @pl.loop(0, CA // 768)
    def _(j):
        part = pl.ds(pl.multiple_of(j * 768, 256), 768)
        rows = reta[:, :, part].reshape(ROWS, 768)
        pool((tok_ref[:, part].astype(f32) + mixture(gates[0], rows)).astype(bf16), part)

    for i in range(PLANE):
        pb[i, :, D:] = count[2 * i : 2 * i + 2]

    for dz, dy in plane:
        target = moved(0, 0, dz, dy)
        copy = remote(pb.at[target[2]], pr.at[me], p_ss.at[target[2]], p_rs.at[me], target)
        copy.start()
        sends.append(copy)
    pr[me] = pb[me]
    for dz, dy in plane:
        target = moved(0, 0, dz, dy)
        remote(pb.at[0], pr.at[target[2]], p_ss.at[0], p_rs.at[target[2]], target).wait_recv()
    p2[...] = jnp.sum(pr[...], axis=0)
    mine = x * 2 + c
    for k, (dx, dc) in enumerate(line):
        target = moved(dx, dc)
        copy = remote(p2, p2r.at[mine], p2_ss.at[k], p2_rs.at[mine], target)
        copy.start()
        sends.append(copy)
    p2r[mine] = p2[...]
    for k, (dx, dc) in enumerate(line):
        target = moved(dx, dc)
        other = target[0] * 2 + target[1]
        remote(p2, p2r.at[other], p2_ss.at[k], p2_rs.at[other], target).wait_recv()
    total = jnp.sum(p2r[...], axis=0)
    p3[me] = total[:, :D] / jnp.concatenate([total[:, D:]] * (D // 128), axis=1)
    for dz, dy in plane:
        target = moved(0, 0, dz, dy)
        copy = remote(p3.at[me], p3.at[me], p3_ss.at[target[2]], p3_rs.at[me], target)
        copy.start()
        sends.append(copy)
    for dz, dy in plane:
        target = moved(0, 0, dz, dy)
        remote(p3.at[target[2]], p3.at[target[2]], p3_ss.at[0], p3_rs.at[target[2]], target).wait_recv()
    for i in range(PLANE):
        pool_ref[2 * i : 2 * i + 2, :] = p3[i]
    for copy in sends:
        copy.wait_send()


def shards(tokens, routes, gates, segments, w_gate, w_up, w_down):
    vmem = pl.BlockSpec(memory_space=pltpu.VMEM)
    hbm = pl.BlockSpec(memory_space=pl.ANY)
    sem = pltpu.SemaphoreType.DMA
    return pl.pallas_call(
        kernel,
        name="moe",
        out_shape=(
            jax.ShapeDtypeStruct((TOK, D), bf16),
            jax.ShapeDtypeStruct((NSEQ, D), f32),
        ),
        in_specs=[vmem] * 4 + [hbm] * 3,
        out_specs=(vmem, vmem),
        scratch_shapes=[
            pltpu.VMEM((EXPERTS, CAP, CA), bf16),
            pltpu.VMEM((EXPERTS, NX, CAP, CB), bf16),
            pltpu.VMEM((3, FFC, D), bf16),
            pltpu.VMEM((PLANE, NX, CAP, CA), bf16),
            pltpu.VMEM((PLANE, NX, CAP, CB), bf16),
            pltpu.VMEM((ROWS, FFC), bf16),
            pltpu.VMEM((PLANE, NX, CAP, CA), bf16),
            pltpu.VMEM((PLANE, NX, CAP, CB), bf16),
            pltpu.VMEM((2, PLANE, CAP, CA), bf16),
            pltpu.VMEM((2, PLANE // 2, CAP, CA), bf16),
            pltpu.VMEM((PLANE, CAP, CA), bf16),
            pltpu.VMEM((PLANE, CAP, CA), bf16),
            pltpu.VMEM((PLANE, NX, CAP, CB), bf16),
            pltpu.VMEM((NX, TOK, CB), bf16),
            pltpu.VMEM((NX, 8, 128), f32),
            pltpu.VMEM((NX, 2, TOK, CB), bf16),
            pltpu.VMEM((PLANE, 2, PW), f32),
            pltpu.VMEM((PLANE, 2, PW), f32),
            pltpu.VMEM((2, PW), f32),
            pltpu.VMEM((8, 2, PW), f32),
            pltpu.VMEM((PLANE, 2, D), f32),
            sem((3,)), sem((3,)), sem((3,)), sem((2,)),
            sem((NX,)), sem((NX,)), sem((NX,)), sem((NX,)),
            sem((PLANE,)), sem((PLANE,)), sem((PLANE,)), sem((PLANE,)),
            sem((NX, NZ)), sem((NX, NZ)), sem((2, NZ)), sem((2, NZ)),
            sem((3, 2, NZ)), sem((3, 2, NZ)),
            sem((PLANE,)), sem((PLANE,)), sem((PLANE,)), sem((PLANE,)),
            sem((NX,)), sem((NX,)),
            sem((PLANE,)), sem((PLANE,)),
            sem((8,)), sem((8,)),
            sem((PLANE,)), sem((PLANE,)),
        ],
        compiler_params=pltpu.CompilerParams(
            collective_id=0, has_side_effects=True, vmem_limit_bytes=58 * 2**20
        ),
    )(
        tokens,
        routes.T,
        gates.T,
        segments[None, :],
        jnp.swapaxes(w_gate[0], 0, 1),
        jnp.swapaxes(w_up[0], 0, 1),
        w_down[0],
    )


def solution(mesh):
    placed = (
        P(("dp", "tensor", "expert"), None),
        P(("dp", "tensor", "expert"), None),
        P(("dp", "tensor", "expert"), None),
        P(("dp", "tensor", "expert")),
        P("expert", None, ("dp", "tensor")),
        P("expert", None, ("dp", "tensor")),
        P("expert", ("dp", "tensor"), None),
    )
    return jax.shard_map(
        shards,
        mesh=mesh,
        in_specs=placed,
        out_specs=(P(("dp", "tensor", "expert"), None), P()),
        check_vma=False,
    )
```

time: 193 us -> 137 us (0.71)
  Pallas kernels: 189 us -> 133 us
    pallas_call x1, Pallas kernels: 189 us -> 133 us  [shards(): pl.pallas_call(kernel, name='moe', out_shape=(jax.ShapeDtypeStruct((TOK,...]
where the time goes in v2:
time: 137 us
  Pallas kernels  133 us (97%)
  local copies, waits for them, and re-layouts  3.39 us (2%)
    pallas_call x1, Pallas kernels, shards(): pl.pallas_call(kernel, name='moe', out_shape=(jax.ShapeDtypeStruct((TOK,...  133 us
    unnamed x2, local copies, waits for them, and re-layouts  3.39 us

profile of v2, /device:TPU:1, one launch (start us, length us, event | category | flops | bytes accessed | tf_op | source)
XLA Modules:
  0.0 137.0 jit_solution(3303578399216481687)
XLA Ops:
  0.6 132.9 %moe.1 = (bf16[64,2304]{1,0:T(8,128)(2,1)}, f32[32,2304]{1,0:T(8,128)}) custom-call(bf16[64,2304]{1,0:T(8,128)(2,1)} %tok_ref.1, s32[2,64]{1,0:T(2,128)} %bitcast.13, f32[2,64]{1,0:T(2,128)} %bitcast.14, s32[1,64]{1,0:T(1,128)} %bitcast.15, bf16[480,2304]{1,0:T(8,128)(2,1)} %bitcast.10, bf16[480,2304]{1,0:T(8,128)(2,1)} %bitcast.11, bf16[480,2304]{1,0:T(8,128)(2,1)} %bitcast.12), custom_call_target="tpu_custom_call" | custom-call | tf_op jit(solution)/shard_map/moe/pallas_call | solution.py:339
  133.6 1.7 %copy.11 = bf16[64,2304]{1,0:T(8,128)(2,1)} copy(bf16[64,2304]{1,0:T(8,128)(2,1)} %get-tuple-element.4) | data formatting | bytes 589824
  135.3 1.7 %copy.12 = f32[32,2304]{1,0:T(8,128)} copy(f32[32,2304]{1,0:T(8,128)} %get-tuple-element.5) | data formatting | bytes 589824

commit v3 on v2

--- a/solution.py
+++ b/solution.py
@@ -42,15 +42,19 @@
     return lax.dot_general(a, b, (dims, ((), ())), preferred_element_type=f32)
 
 
+def tiles(columns):
+    return [(first, min(768, columns - first)) for first in range(0, columns, 768)]
+
+
 def kernel(
     tok_ref, routes_ref, gates_ref, seg_ref, wg_ref, wu_ref, wd_ref, emb_ref, pool_ref,
-    sa, sb, wbuf, ra, rb, hbuf, ta, tb, va, qa, ua, reta, retb, raw, meta, mixed, pb, pr, p2, p2r, p3,
+    sa, sb, wbuf, ra, rb, hbuf, ta, tb, va, qa, ua, reta, retb, raw, meta, mixed, mbs, mbr, ps, pb, pr, p2, p2r, p3,
     w_ls, w_ss, w_rs, l_s, raw_ss, raw_rs, meta_ss, meta_rs, da_ss, da_rs, db_ss, db_rs, x_ss, x_rs, x2_ss, x2_rs,
-    y_ss, y_rs, ba_ss, ba_rs, bb_ss, bb_rs, m_ss, m_rs, p_ss, p_rs, p2_ss, p2_rs, p3_ss, p3_rs,
+    y_ss, y_rs, ba_ss, ba_rs, bb_ss, bb_rs, m_ss, m_rs, mb_ss, mb_rs, o_ss, o_rs, p_ss, p_rs, p2_ss, p2_rs, p3_ss, p3_rs,
 ):
     x, c, z, y = place()
     me = lax.axis_index("expert")
-    plane = [(dz, dy) for dz in (0, 3, 2, 1) for dy in range(NY) if dz or dy]
+    plane = [(2, 2), (3, 2), (2, 3), (1, 2), (2, 1), (2, 0), (0, 2), (1, 1), (3, 3), (1, 3), (3, 1), (1, 0), (0, 3), (3, 0), (0, 1)]
     line = [(dx, dc) for dx in range(NX) for dc in range(2) if dx or dc]
     around = (1, 3, 2)
     sends = []
@@ -60,6 +64,10 @@
             src_ref=src, dst_ref=dst, send_sem=send, recv_sem=recv, device_id=target, device_id_type=MESH
         )
 
+    def home(i):
+        dz, dy = plane[i - 1]
+        return moved(0, 0, NZ - dz, NY - dy)
+
     def give(src, dst, send, recv, target):
         copy = remote(src, dst, send, recv, target)
         copy.start()
@@ -81,53 +89,80 @@
 
     meta[0] = jnp.concatenate(
         [
-            jnp.concatenate([routes_ref[...].astype(f32), gates_ref[...], jnp.zeros((4, TOK), f32)], axis=0),
-            jnp.zeros((8, 128 - TOK), f32),
+            jnp.concatenate(
+                [routes_ref[...].astype(f32), gates_ref[...], seg_ref[...].astype(f32), jnp.zeros((3, TOK), f32)], axis=0
+            ),
+            jnp.full((8, 128 - TOK), -1.0, f32),
         ],
         axis=1,
     )
-    experts = lax.broadcasted_iota(jnp.int32, (EXPERTS, TOK), 0).astype(f32)
-    earlier = lax.broadcasted_iota(jnp.int32, (TOK, TOK), 0) < lax.broadcasted_iota(jnp.int32, (TOK, TOK), 1)
+    experts = lax.broadcasted_iota(jnp.int32, (EXPERTS, 128), 0).astype(f32)
+    earlier = lax.broadcasted_iota(jnp.int32, (128, 128), 0) < lax.broadcasted_iota(jnp.int32, (128, 128), 1)
     earlier = jnp.where(earlier, 1.0, 0.0).astype(bf16)
     slots = lax.broadcasted_iota(jnp.int32, (EXPERTS, CAP, TOK), 1).astype(f32)
 
-    def place_rows(d):
+    def spots_of(d):
         rows = meta[d]
-        named = jnp.where((experts == rows[0:1, :TOK]) | (experts == rows[1:2, :TOK]), 1.0, 0.0)
-        spot = jnp.where(named > 0.5, dot(named.astype(bf16), earlier), -1.0)
-        return jnp.where(slots == spot[:, None, :], 1.0, 0.0).reshape(EXPERTS * CAP, TOK).astype(bf16)
+        named = jnp.where((experts == rows[0:1]) | (experts == rows[1:2]), 1.0, 0.0)
+        return jnp.where(named > 0.5, dot(named.astype(bf16), earlier), -1.0)
+
+    def place_rows(spot):
+        return jnp.where(slots == spot[:, None, :TOK], 1.0, 0.0).reshape(EXPERTS * CAP, TOK).astype(bf16)
 
     values = tok_ref[...].astype(f32)
     scale = lax.rsqrt(jnp.mean(values * values, axis=1, keepdims=True) + epsilon)
     normed = (values * scale).astype(bf16)
     raw[0] = normed[:, CA:]
+    spots = [spots_of(0), None, None, None]
+    placing = place_rows(spots[0])
+    sa[...] = dot(placing, normed[:, :CA]).astype(bf16).reshape(EXPERTS, CAP, CA)
 
     pl.semaphore_wait(barrier, len(plane) + len(line))
     for dx in around:
         d = (NX - dx) % NX
         give(meta.at[0], meta.at[d], meta_ss.at[d], meta_rs.at[d], moved(dx))
         give(raw.at[0], raw.at[d], raw_ss.at[d], raw_rs.at[d], moved(dx))
-    spots = place_rows(0)
-    sa[...] = dot(spots, normed[:, :CA]).astype(bf16).reshape(EXPERTS, CAP, CA)
     own = [pltpu.make_async_copy(sa.at[me // 2], ra.at[0, 0], l_s.at[0])]
     own[0].start()
-    for dz, dy in plane:
+    for back, (dz, dy) in enumerate(plane, 1):
         target = moved(0, 0, dz, dy)
-        back = ((NZ - dz) % NZ) * NY + (NY - dy) % NY
         give(sa.at[target[2] // 2], ra.at[back, 0], da_ss.at[back], da_rs.at[back], target)
+    own[0].wait()
+    for k, (dx, d) in enumerate(((1, 3), (3, 1))):
+        give(ra.at[0, 0], ra.at[0, d], o_ss.at[k], o_rs.at[k], moved(dx))
     for k, w in enumerate(weights):
         give(w, wbuf.at[k, pl.ds(FFD, FFD)], w_ss.at[k], w_rs.at[k], moved(0, 1))
-    sb[:, 0] = dot(spots, raw[0]).astype(bf16).reshape(EXPERTS, CAP, CB)
+    sb[:, 0] = dot(placing, raw[0]).astype(bf16).reshape(EXPERTS, CAP, CB)
     for d in around:
         taken(meta.at[d], meta_rs.at[d])
         taken(raw.at[d], raw_rs.at[d])
-        sb[:, d] = dot(place_rows(d), raw[d]).astype(bf16).reshape(EXPERTS, CAP, CB)
+        spots[d] = spots_of(d)
+        sb[:, d] = dot(place_rows(spots[d]), raw[d]).astype(bf16).reshape(EXPERTS, CAP, CB)
     own.append(pltpu.make_async_copy(sb.at[me // 2], rb.at[0], l_s.at[1]))
     own[1].start()
-    for dz, dy in plane:
+    for back, (dz, dy) in enumerate(plane, 1):
         target = moved(0, 0, dz, dy)
-        back = ((NZ - dz) % NZ) * NY + (NY - dy) % NY
         give(sb.at[target[2] // 2], rb.at[back], db_ss.at[back], db_rs.at[back], target)
+    info = jnp.concatenate([meta[d] for d in range(NX)], axis=1)
+    lane = jnp.concatenate([jnp.where(s < 0.0, s, s + CAP * d) for d, s in enumerate(spots)], axis=1)
+    names = jnp.concatenate([experts] * NX, axis=1)
+    gate = jnp.where(names == info[0:1], info[2:3], 0.0) + jnp.where(names == info[1:2], info[3:4], 0.0)
+    gate_high = gate.astype(bf16).astype(f32)
+    to = lax.broadcasted_iota(jnp.int32, (128, NX * 128), 0).astype(f32)
+    for e in range(EXPERTS):
+        facts = jnp.concatenate(
+            [
+                gate_high[e : e + 1], gate[e : e + 1] - gate_high[e : e + 1], info[4:5],
+                jnp.zeros((5, NX * 128), f32),
+            ],
+            axis=0,
+        ).astype(bf16)
+        hits = jnp.where(to == lane[e : e + 1], 1.0, 0.0).astype(bf16)
+        mbs[e] = dot(facts, hits, ((1,), (1,)))
+    mbr[0] = mbs[me // 2]
+    for back, (dz, dy) in enumerate(plane, 1):
+        target = moved(0, 0, dz, dy)
+        give(mbs.at[target[2] // 2], mbr.at[back], mb_ss.at[back], mb_rs.at[back], target)
     wbuf[:, pl.ds(2 * FFD, FFC - 2 * FFD), :] = jnp.zeros((3, FFC - 2 * FFD, D), bf16)
 
     def four(g):
@@ -135,19 +170,22 @@
 
     def two(g, k):
         return pl.ds(g * NY + 2 * k, 2)
+
+    def fresh(g):
+        return pl.ds(g * NY, NY) if g else pl.ds(1, NY - 1)
 
     def forward(g):
         for i in range(g * NY, (g + 1) * NY):
             if i:
                 taken(ra.at[i, 0], da_rs.at[i])
-            else:
-                own[0].wait()
         for dx, d in ((1, 3), (3, 1)):
-            give(ra.at[four(g), 0], ra.at[four(g), d], x_ss.at[d, g], x_rs.at[d, g], moved(dx))
+            give(ra.at[fresh(g), 0], ra.at[fresh(g), d], x_ss.at[d, g], x_rs.at[d, g], moved(dx))
 
     def relay(g):
         for k, d, dx in ((0, 3, 1), (1, 1, 3)):
-            taken(ra.at[four(g), d], x_rs.at[d, g])
+            taken(ra.at[fresh(g), d], x_rs.at[d, g])
+            if g == 0:
+                taken(ra.at[0, d], o_rs.at[k])
             give(ra.at[two(g, k), d], ra.at[two(g, k), 2], x2_ss.at[k, g], x2_rs.at[k, g], moved(dx))
 
     def ffn(g):
@@ -169,14 +207,26 @@
             up = dot(rows_a, wbuf[1, part, :CA], nt) + dot(rows_b, wbuf[1, part, CA:], nt)
             hbuf[:, part] = (gate / (1.0 + jnp.exp(-gate)) * up).astype(bf16)
 
-        for ref, first, width in ((tb, CA, CB), (ta, 0, CA)):
-            @pl.loop(0, width // 768)
-            def _(j):
-                part = pl.ds(pl.multiple_of(j * 768, 256), 768)
-                down = pl.ds(pl.multiple_of(first + j * 768, 256), 768)
-                ref[g * NY : (g + 1) * NY, :, :, part] = (
-                    dot(hbuf[...], wbuf[2, :, down]).astype(bf16).reshape(NY, NX, CAP, 768)
+        for ref, start, columns in ((tb, CA, CB), (ta, 0, CA)):
+            for first, width in tiles(columns):
+                down = slice(start + first, start + first + width)
+                ref[g * NY : (g + 1) * NY, :, :, first : first + width] = (
+                    dot(hbuf[...], wbuf[2, :, down]).astype(bf16).reshape(NY, NX, CAP, width)
                 )
+
+    sequence = lax.broadcasted_iota(jnp.int32, (NSEQ, 128), 0).astype(f32)
+
+    def per_sequence(g):
+        for i in range(g * NY, (g + 1) * NY):
+            if i:
+                taken(mbr.at[i], mb_rs.at[i])
+            rows = mbr[i]
+            hit = sequence == rows[2:3]
+            weigh = jnp.concatenate([jnp.where(hit, rows[0:1], 0.0), jnp.where(hit, rows[1:2], 0.0)], axis=0)
+            weigh = weigh[:, : NX * CAP].astype(bf16)
+            for ref, part in ((ta, slice(0, CA)), (tb, slice(CA, D))):
+                both = dot(weigh, ref[i].reshape(NX * CAP, ref.shape[3]))
+                ps[:, part] += both[:NSEQ] + both[NSEQ:]
 
     def sums(g):
         for k, dx in ((0, 1), (1, 3)):
@@ -185,7 +235,7 @@
             give(ta.at[two(g, k), d], va.at[v, two(g, k)], y_ss.at[1, v, g], y_rs.at[1, v, g], moved(d))
         for i in range(g * NY, (g + 1) * NY):
             if i:
-                give(tb.at[i], retb.at[me], bb_ss.at[i], bb_rs.at[me], moved(0, 0, i // NY, i % NY))
+                give(tb.at[i], retb.at[me], bb_ss.at[i], bb_rs.at[me], home(i))
             else:
                 retb[me] = tb[0]
 
@@ -206,7 +256,7 @@
             total = (ta[i, 0].astype(f32) + va[0, i].astype(f32) + va[1, i].astype(f32)).astype(bf16)
             if i:
                 ua[i] = total
-                give(ua.at[i], reta.at[me], ba_ss.at[i], ba_rs.at[me], moved(0, 0, i // NY, i % NY))
+                give(ua.at[i], reta.at[me], ba_ss.at[i], ba_rs.at[me], home(i))
             else:
                 reta[me] = total
 
@@ -221,18 +271,32 @@
         copy.wait()
     for k in range(3):
         taken(wbuf.at[k, pl.ds(FFD, FFD)], w_rs.at[k])
+    hot = (lax.broadcasted_iota(jnp.int32, (NSEQ, TOK), 0) == seg_ref[...]).astype(f32)
+    count = jnp.broadcast_to(jnp.sum(hot, axis=1, keepdims=True), (NSEQ, 128))
+    ps[...] = dot(hot.astype(bf16), tok_ref[...])
     ffn(0)
     sums(0)
     relay(3)
+    per_sequence(0)
     ffn(1)
     sums(1)
     pass_on(0)
+    per_sequence(1)
     ffn(2)
     sums(2)
     pass_on(1)
     finish(0)
+    per_sequence(2)
     ffn(3)
     sums(3)
+    per_sequence(3)
+    for i in range(PLANE):
+        pb[i, :, :D] = ps[2 * i : 2 * i + 2, :]
+        pb[i, :, D:] = count[2 * i : 2 * i + 2]
+    for dz, dy in plane:
+        target = moved(0, 0, dz, dy)
+        give(pb.at[target[2]], pr.at[me], p_ss.at[target[2]], p_rs.at[me], target)
+    pr[me] = pb[me]
     pass_on(2)
     finish(1)
 
@@ -257,6 +321,14 @@
         return dot(gate[0], rows) + dot(gate[1], rows)
 
     gates = [gate_rows(d) for d in range(NX)]
+    for dz, dy in plane:
+        other = moved(0, 0, dz, dy)[2]
+        taken(pr.at[other], p_rs.at[other])
+    p2[...] = jnp.sum(pr[...], axis=0)
+    mine = x * 2 + c
+    for k, (dx, dc) in enumerate(line):
+        give(p2, p2r.at[mine], p2_ss.at[k], p2_rs.at[mine], moved(dx, dc))
+    p2r[mine] = p2[...]
     pass_on(3)
     finish(2)
     for dz, dy in plane:
@@ -265,69 +337,33 @@
     for d in around:
         mixed[d, 0] = mixture(gates[d], retb[:, d].reshape(ROWS, CB)).astype(bf16)
         give(mixed.at[d, 0], mixed.at[(NX - d) % NX, 1], m_ss.at[d], m_rs.at[(NX - d) % NX], moved(d))
+    for dx, dc in line:
+        target = moved(dx, dc)
+        other = target[0] * 2 + target[1]
+        taken(p2r.at[other], p2_rs.at[other])
+    total = jnp.sum(p2r[...], axis=0)
+    p3[me] = total[:, :D] / jnp.concatenate([total[:, D:]] * (D // 128), axis=1)
+    for dz, dy in plane:
+        target = moved(0, 0, dz, dy)
+        give(p3.at[me], p3.at[me], p3_ss.at[target[2]], p3_rs.at[me], target)
     finish(3)
     own_mix = mixture(gates[0], retb[:, 0].reshape(ROWS, CB))
-
-    hot = (lax.broadcasted_iota(jnp.int32, (NSEQ, TOK), 0) == seg_ref[...]).astype(f32)
-    count = jnp.broadcast_to(jnp.sum(hot, axis=1, keepdims=True), (NSEQ, 128))
-    hot = hot.astype(bf16)
-
-    def pool(embedded, part):
-        emb_ref[:, part] = embedded
-        sums = dot(hot, embedded)
-        for i in range(PLANE):
-            pb[i, :, part] = sums[2 * i : 2 * i + 2]
-
     for d in around:
         taken(mixed.at[d, 1], m_rs.at[d])
         own_mix = own_mix + mixed[d, 1].astype(f32)
-    pool((tok_ref[:, CA:].astype(f32) + own_mix).astype(bf16), pl.ds(CA, CB))
+    emb_ref[:, CA:] = (tok_ref[:, CA:].astype(f32) + own_mix).astype(bf16)
+    for dz, dy in plane:
+        other = moved(0, 0, dz, dy)[2]
+        taken(p3.at[other], p3_rs.at[other])
+    for i in range(PLANE):
+        pool_ref[2 * i : 2 * i + 2, :] = p3[i]
     for dz, dy in plane:
         other = moved(0, 0, dz, dy)[2]
         taken(reta.at[other], ba_rs.at[other])
-
-    @pl.loop(0, CA // 768)
-    def _(j):
-        part = pl.ds(pl.multiple_of(j * 768, 256), 768)
-        rows = reta[:, :, part].reshape(ROWS, 768)
-        pool((tok_ref[:, part].astype(f32) + mixture(gates[0], rows)).astype(bf16), part)
-
-    for i in range(PLANE):
-        pb[i, :, D:] = count[2 * i : 2 * i + 2]
-
-    for dz, dy in plane:
-        target = moved(0, 0, dz, dy)
-        copy = remote(pb.at[target[2]], pr.at[me], p_ss.at[target[2]], p_rs.at[me], target)
-        copy.start()
-        sends.append(copy)
-    pr[me] = pb[me]
-    for dz, dy in plane:
-        target = moved(0, 0, dz, dy)
-        remote(pb.at[0], pr.at[target[2]], p_ss.at[0], p_rs.at[target[2]], target).wait_recv()
-    p2[...] = jnp.sum(pr[...], axis=0)
-    mine = x * 2 + c
-    for k, (dx, dc) in enumerate(line):
-        target = moved(dx, dc)
-        copy = remote(p2, p2r.at[mine], p2_ss.at[k], p2_rs.at[mine], target)
-        copy.start()
-        sends.append(copy)
-    p2r[mine] = p2[...]
-    for k, (dx, dc) in enumerate(line):
-        target = moved(dx, dc)
-        other = target[0] * 2 + target[1]
-        remote(p2, p2r.at[other], p2_ss.at[k], p2_rs.at[other], target).wait_recv()
-    total = jnp.sum(p2r[...], axis=0)
-    p3[me] = total[:, :D] / jnp.concatenate([total[:, D:]] * (D // 128), axis=1)
-    for dz, dy in plane:
-        target = moved(0, 0, dz, dy)
-        copy = remote(p3.at[me], p3.at[me], p3_ss.at[target[2]], p3_rs.at[me], target)
-        copy.start()
-        sends.append(copy)
-    for dz, dy in plane:
-        target = moved(0, 0, dz, dy)
-        remote(p3.at[target[2]], p3.at[target[2]], p3_ss.at[0], p3_rs.at[target[2]], target).wait_recv()
-    for i in range(PLANE):
-        pool_ref[2 * i : 2 * i + 2, :] = p3[i]
+    for first, width in tiles(CA):
+        part = slice(first, first + width)
+        rows = reta[:, :, part].reshape(ROWS, width)
+        emb_ref[:, part] = (tok_ref[:, part].astype(f32) + mixture(gates[0], rows)).astype(bf16)
     for copy in sends:
         copy.wait_send()
 
@@ -362,6 +398,9 @@
             pltpu.VMEM((NX, TOK, CB), bf16),
             pltpu.VMEM((NX, 8, 128), f32),
             pltpu.VMEM((NX, 2, TOK, CB), bf16),
+            pltpu.VMEM((EXPERTS, 8, 128), f32),
+            pltpu.VMEM((PLANE, 8, 128), f32),
+            pltpu.VMEM((NSEQ, D), f32),
             pltpu.VMEM((PLANE, 2, PW), f32),
             pltpu.VMEM((PLANE, 2, PW), f32),
             pltpu.VMEM((2, PW), f32),
@@ -374,6 +413,7 @@
             sem((3, 2, NZ)), sem((3, 2, NZ)),
             sem((PLANE,)), sem((PLANE,)), sem((PLANE,)), sem((PLANE,)),
             sem((NX,)), sem((NX,)),
+            sem((PLANE,)), sem((PLANE,)), sem((2,)), sem((2,)),
             sem((PLANE,)), sem((PLANE,)),
             sem((8,)), sem((8,)),
             sem((PLANE,)), sem((PLANE,)),

time: 137 us -> 115 us (0.84)
  Pallas kernels: 133 us -> 111 us
    pallas_call x1, Pallas kernels: 133 us -> 111 us  [shards(): pl.pallas_call(kernel, name='moe', out_shape=(jax.ShapeDtypeStruct((TOK,...]
where the time goes in v3:
time: 115 us
  Pallas kernels  111 us (97%)
  local copies, waits for them, and re-layouts  3.39 us (3%)
    pallas_call x1, Pallas kernels, shards(): pl.pallas_call(kernel, name='moe', out_shape=(jax.ShapeDtypeStruct((TOK,...  111 us
    unnamed x2, local copies, waits for them, and re-layouts  3.39 us

profile of v3, /device:TPU:1, one launch (start us, length us, event | category | flops | bytes accessed | tf_op | source)
XLA Modules:
  0.0 115.2 jit_solution(799565715720225851)
XLA Ops:
  0.6 111.1 %moe.1 = (bf16[64,2304]{1,0:T(8,128)(2,1)}, f32[32,2304]{1,0:T(8,128)}) custom-call(bf16[64,2304]{1,0:T(8,128)(2,1)} %tok_ref.1, s32[2,64]{1,0:T(2,128)} %bitcast.13, f32[2,64]{1,0:T(2,128)} %bitcast.14, s32[1,64]{1,0:T(1,128)} %bitcast.15, bf16[480,2304]{1,0:T(8,128)(2,1)} %bitcast.10, bf16[480,2304]{1,0:T(8,128)(2,1)} %bitcast.11, bf16[480,2304]{1,0:T(8,128)(2,1)} %bitcast.12), custom_call_target="tpu_custom_call" | custom-call | tf_op jit(solution)/shard_map/moe/pallas_call | solution.py:375
  111.8 1.7 %copy.11 = bf16[64,2304]{1,0:T(8,128)(2,1)} copy(bf16[64,2304]{1,0:T(8,128)(2,1)} %get-tuple-element.4) | data formatting | bytes 589824
  113.5 1.7 %copy.12 = f32[32,2304]{1,0:T(8,128)} copy(f32[32,2304]{1,0:T(8,128)} %get-tuple-element.5) | data formatting | bytes 589824

commit v4 on v3

--- a/solution.py
+++ b/solution.py
@@ -54,7 +54,7 @@
 ):
     x, c, z, y = place()
     me = lax.axis_index("expert")
-    plane = [(2, 2), (3, 2), (2, 3), (1, 2), (2, 1), (2, 0), (0, 2), (1, 1), (3, 3), (1, 3), (3, 1), (1, 0), (0, 3), (3, 0), (0, 1)]
+    plane = [(1, 1), (3, 3), (2, 2), (1, 3), (3, 1), (2, 0), (0, 2), (3, 2), (2, 3), (1, 2), (2, 1), (1, 0), (0, 3), (3, 0), (0, 1)]
     line = [(dx, dc) for dx in range(NX) for dc in range(2) if dx or dc]
     around = (1, 3, 2)
     sends = []
@@ -140,9 +140,13 @@
         sb[:, d] = dot(place_rows(spots[d]), raw[d]).astype(bf16).reshape(EXPERTS, CAP, CB)
     own.append(pltpu.make_async_copy(sb.at[me // 2], rb.at[0], l_s.at[1]))
     own[1].start()
-    for back, (dz, dy) in enumerate(plane, 1):
-        target = moved(0, 0, dz, dy)
-        give(sb.at[target[2] // 2], rb.at[back], db_ss.at[back], db_rs.at[back], target)
+    def offer(g):
+        for back in range(max(1, g * NY), (g + 1) * NY):
+            target = moved(0, 0, *plane[back - 1])
+            give(sb.at[target[2] // 2], rb.at[back], db_ss.at[back], db_rs.at[back], target)
+
+    offer(0)
+    offer(1)
     info = jnp.concatenate([meta[d] for d in range(NX)], axis=1)
     lane = jnp.concatenate([jnp.where(s < 0.0, s, s + CAP * d) for d, s in enumerate(spots)], axis=1)
     names = jnp.concatenate([experts] * NX, axis=1)
@@ -262,8 +266,10 @@
 
     forward(0)
     forward(1)
+    offer(2)
     relay(0)
     forward(2)
+    offer(3)
     relay(1)
     forward(3)
     relay(2)

time: 115 us -> 112 us (0.974)
  Pallas kernels: 111 us -> 108 us
    pallas_call x1, Pallas kernels: 111 us -> 108 us  [shards(): pl.pallas_call(kernel, name='moe', out_shape=(jax.ShapeDtypeStruct((TOK,...]
where the time goes in v4:
time: 112 us
  Pallas kernels  108 us (96%)
  local copies, waits for them, and re-layouts  3.39 us (3%)
    pallas_call x1, Pallas kernels, shards(): pl.pallas_call(kernel, name='moe', out_shape=(jax.ShapeDtypeStruct((TOK,...  108 us
    unnamed x2, local copies, waits for them, and re-layouts  3.39 us

profile of v4, /device:TPU:1, one launch (start us, length us, event | category | flops | bytes accessed | tf_op | source)
XLA Modules:
  0.0 112.2 jit_solution(17926537715735005659)
XLA Ops:
  0.6 108.2 %moe.1 = (bf16[64,2304]{1,0:T(8,128)(2,1)}, f32[32,2304]{1,0:T(8,128)}) custom-call(bf16[64,2304]{1,0:T(8,128)(2,1)} %tok_ref.1, s32[2,64]{1,0:T(2,128)} %bitcast.13, f32[2,64]{1,0:T(2,128)} %bitcast.14, s32[1,64]{1,0:T(1,128)} %bitcast.15, bf16[480,2304]{1,0:T(8,128)(2,1)} %bitcast.10, bf16[480,2304]{1,0:T(8,128)(2,1)} %bitcast.11, bf16[480,2304]{1,0:T(8,128)(2,1)} %bitcast.12), custom_call_target="tpu_custom_call" | custom-call | tf_op jit(solution)/shard_map/moe/pallas_call | solution.py:381
  108.8 1.7 %copy.11 = bf16[64,2304]{1,0:T(8,128)(2,1)} copy(bf16[64,2304]{1,0:T(8,128)(2,1)} %get-tuple-element.4) | data formatting | bytes 589824
  110.5 1.7 %copy.12 = f32[32,2304]{1,0:T(8,128)} copy(f32[32,2304]{1,0:T(8,128)} %get-tuple-element.5) | data formatting | bytes 589824
